TPU v7x, 32 devices: a whole 2x2x4 slice. The times are simulated.
32 devices in a mesh: row: 8 (over z, x), col: 4 (over y, core).
Axes of the slice: x: 2, y: 2, z: 4, core: 2. Of those that a mesh axis runs over, the one named last changes fastest.
Arguments:
- input_picture: bfloat16 [128, 512, 256], P('row', 'col'), may hold values from -6 to 6
- spatial_taps_first: bfloat16 [2, 49, 256], replicated, may hold values from -0.875 to 0.875
- widening_matrix_first: bfloat16 [2, 256, 1024], replicated, may hold values from -0.375 to 0.375
- narrowing_matrix_first: bfloat16 [2, 1024, 256], replicated, may hold values from -0.1875 to 0.1875
- stride_kernel_matrix: bfloat16 [1024, 512], replicated, may hold values from -0.1875 to 0.1875
- spatial_taps_second: bfloat16 [2, 49, 512], replicated, may hold values from -0.875 to 0.875
- widening_matrix_second: bfloat16 [2, 512, 2048], replicated, may hold values from -0.25 to 0.25
- narrowing_matrix_second: bfloat16 [2, 2048, 512], replicated, may hold values from -0.125 to 0.125
- sky_clarity_marks: int32 [1, 4], replicated, may hold values 0 or 1
Outputs:
- features: bfloat16 [64, 256, 512], P('row', 'col')
Inputs may be any that keep to these rules, and one draw needn't show every extreme that they name: `sky_clarity_marks`: 1 marks a tile of 64 x 64 section-two pixels whose blocks are applied, 0 a cloudy tile that passes through section two unchanged.
All inputs are finite; a program needn't handle non-finite values.
Results may differ from a plain program's by a relative error of at most 0.022.
Values may be sent and summed in bfloat16 or wider, within the bound.
A program may use at most 128 MiB of HBM per device.

v0:
```python
import functools

import jax
import jax.numpy as jnp
from jax import lax
from jax.experimental import pallas as pl
from jax.experimental.pallas import tpu as pltpu
from jax.sharding import PartitionSpec as P

TILE2 = 64
EPSILON = 1e-06
HALO = 3
COLS = 16
ERF_FIT = (0.7976901192585555, 0.03673081477632814, -0.0002550994688061032, -8.607627436402819e-06)
ERF_END = 25.0
SIDES = ((-1, 0), (1, 0), (0, -1), (0, 1), (-1, -1), (-1, 1), (1, -1), (1, 1))
f32 = jnp.float32
bf16 = jnp.bfloat16


def first_block(tap_col):
    return 0 if tap_col < 3 else 1


def tap_blocks(tap_col, wide):
    return wide if tap_col == 3 else wide + 1


def slot_offset(tap_col, wide):
    return sum(tap_blocks(b, wide) for b in range(tap_col))


def kernel(
    count_rows,
    count_cols,
    x_hbm, t1_hbm, a1_hbm, b1_hbm, sk_hbm, t2_hbm, a2_hbm, b2_hbm, flag_ref,
    out_ref,
    x0, x1, z0, z1, t1, a1, b1, sk, t2, a2, b2,
    kb1, kb2, sum1, sum2, shift1, shift2, split, patches,
    load_sem, send_sem, recv_sem,
):
    rows_one = x0.shape[0] - 2 * HALO
    rows_two = z0.shape[0] - 2 * HALO
    wide_one = x0.shape[1] - 2
    wide_two = z0.shape[1] - 2
    c_one = x0.shape[-1]
    c_two = z0.shape[-1]
    me_row = lax.axis_index("row")
    me_col = lax.axis_index("col")

    def exists(dr, dc):
        ok = None
        for step, me, count in ((dr, me_row, count_rows), (dc, me_col, count_cols)):
            if step == 0:
                continue
            here = me > 0 if step < 0 else me < count - 1
            ok = here if ok is None else jnp.logical_and(ok, here)
        return ok

    loads = []
    for index, (src, dst) in enumerate(
        (
            (x_hbm, x0.at[pl.ds(HALO, rows_one), pl.ds(1, wide_one)]),
            (t1_hbm, t1), (a1_hbm, a1), (b1_hbm, b1),
            (sk_hbm, sk), (t2_hbm, t2), (a2_hbm, a2), (b2_hbm, b2),
        )
    ):
        copy = pltpu.make_async_copy(src, dst, load_sem.at[index])
        copy.start()
        loads.append(copy)

    barrier = pltpu.get_barrier_semaphore()
    total = jnp.int32(0)
    for dr, dc in SIDES:
        near = exists(dr, dc)

        @pl.when(near)
        def _(dr=dr, dc=dc):
            pl.semaphore_signal(
                barrier, inc=1, device_id=(me_row + dr, me_col + dc), device_id_type=pl.DeviceIdType.MESH
            )

        total = total + jnp.where(near, 1, 0)
    pl.semaphore_wait(barrier, total)

    def transfer(which, side, source=None):
        dr, dc = SIDES[side]
        field = (x0, x1, z0, z1)[which]
        rows = field.shape[0] - 2 * HALO
        wide = field.shape[1] - 2
        from_row = {-1: 0, 0: 0, 1: rows - HALO}[dr]
        to_row = {-1: HALO + rows, 0: HALO, 1: 0}[dr]
        n_rows = HALO if dr else rows
        from_block = {-1: 0, 0: 0, 1: wide - 1}[dc]
        to_block = {-1: wide + 1, 0: 1, 1: 0}[dc]
        n_blocks = 1 if dc else wide
        if source is None:
            src = field.at[pl.ds(HALO + from_row, n_rows), pl.ds(1 + from_block, n_blocks)]
        else:
            src = source.at[pl.ds(from_row, n_rows), pl.ds(from_block, n_blocks)]
        return pltpu.make_async_remote_copy(
            src_ref=src,
            dst_ref=field.at[pl.ds(to_row, n_rows), pl.ds(to_block, n_blocks)],
            send_sem=send_sem.at[which, side],
            recv_sem=recv_sem.at[which, side],
            device_id=(
                jnp.clip(me_row + dr, 0, count_rows - 1),
                jnp.clip(me_col + dc, 0, count_cols - 1),
            ),
            device_id_type=pl.DeviceIdType.MESH,
        )

    def send(which, sides, source=None):
        for side in sides:
            @pl.when(exists(*SIDES[side]))
            def _(side=side):
                transfer(which, side, source).start()

    def arrive(which, sides):
        for side in sides:
            dr, dc = SIDES[side]

            @pl.when(exists(-dr, -dc))
            def _(side=side):
                transfer(which, side).wait_recv()

    def sent(which, source=None):
        for side in range(len(SIDES)):
            @pl.when(exists(*SIDES[side]))
            def _(side=side):
                transfer(which, side, source).wait_send()

    COLUMN_SIDES = (2, 3)
    OTHER_SIDES = (0, 1, 4, 5, 6, 7)
    send(0, COLUMN_SIDES + OTHER_SIDES, x_hbm)

    for field in (x0, x1, z0, z1):
        rows = field.shape[0] - 2 * HALO
        wide = field.shape[1] - 2
        row_band = jnp.zeros((HALO,) + field.shape[1:], bf16)
        col_band = jnp.zeros((field.shape[0],) + field.shape[2:], bf16)

        @pl.when(me_row == 0)
        def _(field=field, row_band=row_band):
            field[0:HALO] = row_band

        @pl.when(me_row == count_rows - 1)
        def _(field=field, row_band=row_band, rows=rows):
            field[HALO + rows : 2 * HALO + rows] = row_band

        @pl.when(me_col == 0)
        def _(field=field, col_band=col_band):
            field[:, 0] = col_band

        @pl.when(me_col == count_cols - 1)
        def _(field=field, col_band=col_band, wide=wide):
            field[:, wide + 1] = col_band

    def build_shift(ref, wide):
        shape = ref.shape
        gap = lax.broadcasted_iota(jnp.int32, shape, 1) - lax.broadcasted_iota(jnp.int32, shape, 0)
        hit = jnp.zeros(shape, f32)
        for b in range(7):
            start = (slot_offset(b, wide) - first_block(b)) * COLS + COLS - HALO + b
            hit = jnp.where(gap == start, 1.0, hit)
        ref[...] = hit.astype(bf16)

    build_shift(shift1, wide_one)
    build_shift(shift2, wide_two)
    width = split.shape[0]
    target = lax.broadcasted_iota(jnp.int32, split.shape, 0)
    picked = jnp.where(target < width // 2, 2 * target, 2 * target - width + 1)
    split[...] = jnp.where(lax.broadcasted_iota(jnp.int32, split.shape, 1) == picked, 1.0, 0.0).astype(bf16)

    def spread_taps(dst, src):
        for layer in range(src.shape[0]):
            wide_taps = src[layer].astype(f32)
            for tap in range(49):
                dst[layer, tap] = jnp.broadcast_to(wide_taps[tap : tap + 1], dst.shape[2:]).astype(bf16)

    def centre(values):
        c = values.shape[-1]
        ones = jnp.full((c, c), 1.0 / c, bf16)
        mean = jnp.dot(values.astype(bf16), ones, preferred_element_type=f32)
        centred = values - mean
        variance = jnp.dot((centred * centred).astype(bf16), ones, preferred_element_type=f32)
        return (centred * lax.rsqrt(variance + EPSILON)).astype(bf16)

    def gelu_twice(h):
        square = jnp.minimum(h * h, ERF_END)
        q = ERF_FIT[3]
        for term in ERF_FIT[2::-1]:
            q = q * square + term
        return h + h * jnp.tanh(h * q)

    def branch_rows(field, taps, w_in, w_out, sums, shift, layer, row, n):
        wide = field.shape[1] - 2
        c = field.shape[-1]

        def one_block(block, taps_in_row):
            for lane in range(c // 128):
                lanes = slice(lane * 128, (lane + 1) * 128)
                cells = [field[row + r, block, :, lanes] for r in range(n + 2 * HALO)]
                for b in taps_in_row:
                    tap = [taps[layer, 7 * a + b, :, lanes] for a in range(7)]
                    for r in range(n):
                        p = [cells[r + a] * tap[a] for a in range(7)]
                        total = ((p[0] + p[1]) + (p[2] + p[3])) + ((p[4] + p[5]) + p[6])
                        sums[r, slot_offset(b, wide) - first_block(b) + block, :, lanes] = total

        one_block(0, range(0, 3))
        one_block(wide + 1, range(4, 7))

        @pl.loop(1, wide + 1)
        def _(block):
            one_block(block, range(7))

        slots = slot_offset(7, wide)
        mixed = [
            jnp.dot(shift[...], sums[r].reshape(slots * COLS, c), preferred_element_type=f32)
            for r in range(n)
        ]
        flat = centre(jnp.concatenate(mixed, axis=0))
        hidden_size = w_in.shape[-1]
        step = 512
        total = None
        for k in range(0, hidden_size, step):
            h = jnp.dot(flat, w_in[layer, :, k : k + step], preferred_element_type=f32)
            g = gelu_twice(h).astype(bf16)
            part = jnp.dot(g, w_out[layer, k : k + step, :], preferred_element_type=f32)
            total = part if total is None else total + part
        return 0.5 * total

    def plain(field, row, n):
        wide = field.shape[1] - 2
        c = field.shape[-1]
        return field[pl.ds(HALO + row, n), 1 : 1 + wide].astype(f32).reshape(n * wide * COLS, c)

    def section_one(layer, row, n):
        field = (x0, x1)[layer]
        branch = branch_rows(field, kb1, a1, b1, sum1, shift1, layer, row, n)
        new = (plain(field, row, n) + branch).astype(bf16)
        if layer == 0:
            x1[pl.ds(HALO + row, n), 1 : 1 + wide_one] = new.reshape(n, wide_one, COLS, c_one)
        else:
            normed = centre(new.astype(f32))
            for r in range(n):
                both = jnp.dot(
                    split[...], normed[r * width : (r + 1) * width], preferred_element_type=f32
                ).astype(bf16)
                place = row + r
                first = 2 * lax.rem(place, 2)
                patches[first, lax.div(place, 2)] = both[: width // 2]
                patches[first + 1, lax.div(place, 2)] = both[width // 2 :]

    def section_two(layer, row, n):
        field = (z0, z1)[layer]
        branch = branch_rows(field, kb2, a2, b2, sum2, shift2, layer, row, n)
        old = plain(field, row, n)
        keep = jnp.broadcast_to(flag_ref[0:1, :], old.shape) > 0.5
        new = jnp.where(keep, old + branch, old).astype(bf16).reshape(n, wide_two, COLS, c_two)
        if layer == 0:
            z1[pl.ds(HALO + row, n), 1 : 1 + wide_two] = new
        else:
            out_ref[pl.ds(row, n)] = new

    def run(work, which, layer, rows, per_step):
        arrive(which, COLUMN_SIDES)

        @pl.loop(0, (rows - 2 * HALO) // per_step)
        def _(index):
            work(layer, HALO + index * per_step, per_step)

        arrive(which, OTHER_SIDES)

        @pl.loop(0, 2)
        def _(index):
            work(layer, index * (rows - HALO), HALO)

    loads[1].wait()
    spread_taps(kb1, t1)
    loads[0].wait()
    loads[2].wait()
    loads[3].wait()
    run(section_one, 0, 0, rows_one, 2)
    send(1, COLUMN_SIDES + OTHER_SIDES)
    loads[5].wait()
    spread_taps(kb2, t2)
    run(section_one, 1, 1, rows_one, 2)

    loads[4].wait()
    together = 4 if rows_two % 4 == 0 else 1

    @pl.loop(0, rows_two // together)
    def _(index):
        total = None
        for q in range(4):
            patch = patches[q, pl.ds(index * together, together)].reshape(together * (width // 2), c_one)
            part = jnp.dot(patch, sk[q * c_one : (q + 1) * c_one], preferred_element_type=f32)
            total = part if total is None else total + part
        z0[pl.ds(HALO + index * together, together), 1 : 1 + wide_two] = total.astype(bf16).reshape(
            together, wide_two, COLS, c_two
        )

    send(2, COLUMN_SIDES + OTHER_SIDES)
    loads[6].wait()
    loads[7].wait()
    run(section_two, 2, 0, rows_two, 2)
    send(3, COLUMN_SIDES + OTHER_SIDES)
    run(section_two, 3, 1, rows_two, 2)
    sent(0, x_hbm)
    for which in range(1, 4):
        sent(which)


def per_device(
    count_rows,
    count_cols,
    input_picture,
    spatial_taps_first,
    widening_matrix_first,
    narrowing_matrix_first,
    stride_kernel_matrix,
    spatial_taps_second,
    widening_matrix_second,
    narrowing_matrix_second,
    sky_clarity_marks,
):
    rows, cols, c_one = input_picture.shape
    c_two = stride_kernel_matrix.shape[1]
    wide_one = cols // COLS
    wide_two = cols // (2 * COLS)
    tile_row = lax.axis_index("row") * (rows // 2) // TILE2
    tile_col = lax.axis_index("col") * (cols // 2) // TILE2
    flag = lax.dynamic_slice(sky_clarity_marks, (tile_row, tile_col), (1, 1))
    flag = jnp.broadcast_to((flag == 1).astype(f32), (8, c_two))
    slots_one = slot_offset(7, wide_one)
    slots_two = slot_offset(7, wide_two)
    weights = (
        spatial_taps_first, widening_matrix_first, narrowing_matrix_first, stride_kernel_matrix,
        spatial_taps_second, widening_matrix_second, narrowing_matrix_second,
    )
    vmem = pltpu.VMEM
    out = pl.pallas_call(
        functools.partial(kernel, count_rows, count_cols),
        out_shape=jax.ShapeDtypeStruct((rows // 2, wide_two, COLS, c_two), bf16),
        in_specs=[pl.BlockSpec(memory_space=pl.ANY)] * 8 + [pl.BlockSpec(memory_space=vmem)],
        out_specs=pl.BlockSpec(memory_space=vmem),
        scratch_shapes=[
            vmem((rows + 2 * HALO, wide_one + 2, COLS, c_one), bf16),
            vmem((rows + 2 * HALO, wide_one + 2, COLS, c_one), bf16),
            vmem((rows // 2 + 2 * HALO, wide_two + 2, COLS, c_two), bf16),
            vmem((rows // 2 + 2 * HALO, wide_two + 2, COLS, c_two), bf16),
            *[vmem(w.shape, bf16) for w in weights],
            vmem(spatial_taps_first.shape[:2] + (COLS, c_one), bf16),
            vmem(spatial_taps_second.shape[:2] + (COLS, c_two), bf16),
            vmem((HALO, slots_one, COLS, c_one), bf16),
            vmem((HALO, slots_two, COLS, c_two), bf16),
            vmem((cols, slots_one * COLS), bf16),
            vmem((cols // 2, slots_two * COLS), bf16),
            vmem((cols, cols), bf16),
            vmem((4, rows // 2, cols // 2, c_one), bf16),
            pltpu.SemaphoreType.DMA((8,)),
            pltpu.SemaphoreType.DMA((4, len(SIDES))),
            pltpu.SemaphoreType.DMA((4, len(SIDES))),
        ],
        compiler_params=pltpu.CompilerParams(
            collective_id=0, has_side_effects=True, vmem_limit_bytes=60 * 2**20
        ),
        name="sections",
    )(input_picture.reshape(rows, wide_one, COLS, c_one), *weights, flag)
    return out.reshape(rows // 2, cols // 2, c_two)


def solution(mesh):
    placed = (P("row", "col", None), P(), P(), P(), P(), P(), P(), P(), P())
    return jax.shard_map(
        functools.partial(per_device, mesh.shape["row"], mesh.shape["col"]),
        mesh=mesh, in_specs=placed, out_specs=P("row", "col", None), check_vma=False,
    )
```

profile of v0, /device:TPU:11, one launch (start us, length us, event | category | flops | bytes accessed | tf_op | source)
XLA Modules:
  0.0 97.7 jit_solution(11055804207894168591)
XLA Ops:
  0.0 1.2 %fusion = pred[1,1]{1,0:T(4,128)(4,1)} fusion(s32[1,4]{1,0:T(1,128)} %param.17, s32[]{:T(128)S(6)} %select_n.11), kind=kLoop, calls=%fused_computation.1 | loop fusion | flops 1 | bytes 9 | tf_op jit(solution)/shard_map/eq | solution.py:336
  1.9 0.6 broadcast_in_dim.12.flag_ref
  2.5 1.4 %copy.10.t1_hbm = bf16[2,49,256]{2,1,0:T(8,128)(2,1)} copy(bf16[2,49,256]{2,0,1:T(2,128)(2,1)} %param.10) | data formatting | bytes 100352 | tf_op args[1]
  3.9 1.6 %copy.11.t2_hbm = bf16[2,49,512]{2,1,0:T(8,128)(2,1)} copy(bf16[2,49,512]{2,0,1:T(2,128)(2,1)} %param.14) | data formatting | bytes 200704 | tf_op args[5]
  5.5 90.3 %sections.1 = bf16[8,4,16,512]{3,2,1,0:T(8,128)(2,1)} custom-call(bf16[16,8,16,256]{3,2,1,0:T(8,128)(2,1)} %bitcast.4, bf16[2,49,256]{2,1,0:T(8,128)(2,1)} %copy.10.t1_hbm, bf16[2,256,1024]{2,1,0:T(8,128)(2,1)} %a1_hbm.1, bf16[2,1024,256]{2,1,0:T(8,128)(2,1)} %b1_hbm.1, bf16[1024,512]{1,0:T(8,128)(2,1)} %sk_hbm.1, bf16[2,49,512]{2,1,0:T(8,128)(2,1)} %copy.11.t2_hbm, ...), custom_call_target="tpu_custom_call" | custom-call | tf_op jit(solution)/shard_map/sections/pallas_call | solution.py:344
  95.8 1.9 %copy.13 = bf16[8,64,512]{2,1,0:T(8,128)(2,1)} copy(bf16[8,64,512]{2,1,0:T(8,128)(2,1)} %bitcast.3) | data formatting | bytes 1048576
where the time goes:
time: 98 us; the launch traced here: 97.7 us
  Pallas kernels  90.3 us (92%)
  local copies, waits for them, and re-layouts  5.46 us (6%)
  other arithmetic  1.24 us (1%)
    pallas_call x1, Pallas kernels, per_device(): pl.pallas_call(functools.partial(kernel, count_rows, count_cols), out_sha...  90.3 us
    unnamed x3, local copies, waits for them, and re-layouts  4.87 us

commit v1 on v0

v1 whole, which is shorter than its diff:
```python
import functools

import jax
import jax.numpy as jnp
from jax import lax
from jax.experimental import pallas as pl
from jax.experimental.pallas import tpu as pltpu
from jax.sharding import PartitionSpec as P

TILE2 = 64
EPSILON = 1e-06
HALO = 3
COLS = 16
ERF_FIT = (0.7975078823814434, 0.037005647651999776, -0.00035151703937969365)
ERF_END = 25.0
SIDES = ((-1, 0), (1, 0), (0, -1), (0, 1), (-1, -1), (-1, 1), (1, -1), (1, 1))
f32 = jnp.float32
bf16 = jnp.bfloat16


def largest_divisor(number, limit):
    return next(d for d in range(limit, 0, -1) if number % d == 0)


def kernel(
    count_rows,
    count_cols,
    x_hbm, t1_hbm, a1_hbm, b1_hbm, sk_hbm, t2_hbm, a2_hbm, b2_hbm, marks,
    out_ref,
    natural, e0, e1, e2, e3, h1, h2, h3, p1, p2, p3,
    t1, a1, b1, sk, t2, a2, b2,
    kb1, kb2, sum1, sum2,
    order0, fill1, fill2, pack1, pack2, unorder, patches,
    load_sem, send_sem, recv_sem,
):
    fields = (e0, e1, e2, e3)
    edges = (None, h1, h2, h3)
    packs = (None, p1, p2, p3)
    rows_one = e0.shape[0] - 2 * HALO
    rows_two = e2.shape[0] - 2 * HALO
    wide_one = e0.shape[1] - 2 * HALO
    wide_two = e2.shape[1] - 2 * HALO
    c_one = e0.shape[-1]
    c_two = e2.shape[-1]
    me_row = lax.axis_index("row")
    me_col = lax.axis_index("col")

    def exists(dr, dc):
        ok = None
        for step, me, count in ((dr, me_row, count_rows), (dc, me_col, count_cols)):
            if step == 0:
                continue
            here = me > 0 if step < 0 else me < count - 1
            ok = here if ok is None else jnp.logical_and(ok, here)
        return ok

    loads = []
    for index, (src, dst) in enumerate(
        (
            (x_hbm, natural.at[pl.ds(HALO, rows_one), pl.ds(1, wide_one)]),
            (t1_hbm, t1), (a1_hbm, a1), (b1_hbm, b1),
            (sk_hbm, sk), (t2_hbm, t2), (a2_hbm, a2), (b2_hbm, b2),
        )
    ):
        copy = pltpu.make_async_copy(src, dst, load_sem.at[index])
        copy.start()
        loads.append(copy)

    barrier = pltpu.get_barrier_semaphore()
    total = jnp.int32(0)
    for dr, dc in SIDES:
        near = exists(dr, dc)

        @pl.when(near)
        def _(dr=dr, dc=dc):
            pl.semaphore_signal(
                barrier, inc=1, device_id=(me_row + dr, me_col + dc), device_id_type=pl.DeviceIdType.MESH
            )

        total = total + jnp.where(near, 1, 0)
    pl.semaphore_wait(barrier, total)

    def transfer(which, side):
        dr, dc = SIDES[side]
        rows = fields[which].shape[0] - 2 * HALO
        wide = fields[which].shape[1] - 2 * HALO
        from_row = {-1: 0, 0: 0, 1: rows - HALO}[dr]
        to_row = {-1: HALO + rows, 0: HALO, 1: 0}[dr]
        n_rows = HALO if dr else rows
        if which == 0:
            from_block = {-1: 0, 0: 0, 1: wide - 1}[dc]
            to_block = {-1: wide + 1, 0: 1, 1: 0}[dc]
            n_blocks = 1 if dc else wide
            src = x_hbm.at[pl.ds(from_row, n_rows), pl.ds(from_block, n_blocks)]
            dst = natural.at[pl.ds(to_row, n_rows), pl.ds(to_block, n_blocks)]
        elif dc == 0:
            src = fields[which].at[pl.ds(HALO + from_row, n_rows), pl.ds(HALO, wide)]
            dst = fields[which].at[pl.ds(to_row, n_rows), pl.ds(HALO, wide)]
        else:
            src = packs[which].at[pl.ds(from_row, n_rows), pl.ds((1 + dc) // 2, 1)]
            dst = edges[which].at[pl.ds(to_row, n_rows), pl.ds((1 - dc) // 2, 1)]
        return pltpu.make_async_remote_copy(
            src_ref=src,
            dst_ref=dst,
            send_sem=send_sem.at[which, side],
            recv_sem=recv_sem.at[which, side],
            device_id=(
                jnp.clip(me_row + dr, 0, count_rows - 1),
                jnp.clip(me_col + dc, 0, count_cols - 1),
            ),
            device_id_type=pl.DeviceIdType.MESH,
        )

    def send(which):
        for side in (2, 3, 0, 1, 4, 5, 6, 7):
            @pl.when(exists(*SIDES[side]))
            def _(side=side):
                transfer(which, side).start()

    def arrive(which, sides):
        for side in sides:
            dr, dc = SIDES[side]

            @pl.when(exists(-dr, -dc))
            def _(side=side):
                transfer(which, side).wait_recv()

    def sent(which):
        for side in range(len(SIDES)):
            @pl.when(exists(*SIDES[side]))
            def _(side=side):
                transfer(which, side).wait_send()

    send(0)

    for field, left, right, inner in (
        (natural, 0, wide_one + 1, None),
        (h1, 0, 1, e1), (h2, 0, 1, e2), (h3, 0, 1, e3),
    ):
        rows = field.shape[0] - 2 * HALO
        row_band = jnp.zeros((HALO,) + field.shape[1:], bf16)
        col_band = jnp.zeros((field.shape[0],) + field.shape[2:], bf16)

        def clear_rows(first, field=field, inner=inner, row_band=row_band):
            field[first : first + HALO] = row_band
            if inner is not None:
                inner[first : first + HALO] = jnp.zeros((HALO,) + inner.shape[1:], bf16)

        @pl.when(me_row == 0)
        def _(clear_rows=clear_rows):
            clear_rows(0)

        @pl.when(me_row == count_rows - 1)
        def _(clear_rows=clear_rows, rows=rows):
            clear_rows(HALO + rows)

        @pl.when(me_col == 0)
        def _(field=field, col_band=col_band, left=left):
            field[:, left] = col_band

        @pl.when(me_col == count_cols - 1)
        def _(field=field, col_band=col_band, right=right):
            field[:, right] = col_band

    def pick(ref, source):
        wanted = source(lax.broadcasted_iota(jnp.int32, ref.shape, 0))
        column = lax.broadcasted_iota(jnp.int32, ref.shape, 1)
        ref[...] = jnp.where(column == wanted, 1.0, 0.0).astype(bf16)

    def slab_order(m):
        return (m & (COLS - 1)) * wide_one + (m >> 4) - HALO + COLS

    def fill_order(wide):
        def source(m):
            k, s = m >> 4, m & (COLS - 1)
            left = jnp.where(s == 0, wide * COLS + k, (wide - HALO + k) * COLS + s - 1)
            other = k - HALO
            right = jnp.where(s == COLS - 1, (wide + 1) * COLS + other, other * COLS + s + 1)
            return jnp.where(k < HALO, left, right)

        return source

    def pack_order(wide):
        def source(m):
            k = m & (COLS - 1)
            place = jnp.where(m < COLS, k * COLS, (wide - HALO + k) * COLS + COLS - 1)
            return jnp.where(k < HALO, place, -1)

        return source

    def natural_order(m):
        bits = wide_two.bit_length() - 1
        return (m & (wide_two - 1)) * COLS + (m >> bits)

    pick(order0, slab_order)
    pick(fill1, fill_order(wide_one))
    pick(fill2, fill_order(wide_two))
    pick(pack1, pack_order(wide_one))
    pick(pack2, pack_order(wide_two))
    pick(unorder, natural_order)

    def move(matrix, values):
        return jnp.dot(matrix[...], values, preferred_element_type=f32).astype(bf16)

    def spread_taps(dst, src):
        for tap in range(49):
            both = src[tap].astype(f32)
            for layer in range(both.shape[0]):
                dst[layer, tap] = jnp.broadcast_to(both[layer : layer + 1], dst.shape[2:]).astype(bf16)

    def fill(which, row):
        field = fields[which]
        wide = field.shape[1] - 2 * HALO
        c = field.shape[-1]
        if which == 0:
            values = natural[row].reshape((wide + 2) * COLS, c)
            field[row] = move(order0, values).reshape(wide + 2 * HALO, COLS, c)
            return
        inner = field[row, HALO : HALO + wide].reshape(wide * COLS, c)
        values = jnp.concatenate([inner, edges[which][row].reshape(2 * COLS, c)], axis=0)
        outer = move(fill1 if which == 1 else fill2, values).reshape(2 * HALO, COLS, c)
        field[row, 0:HALO] = outer[:HALO]
        field[row, HALO + wide : 2 * HALO + wide] = outer[HALO:]

    def store_field(which, row, n, new):
        field = fields[which]
        wide = field.shape[1] - 2 * HALO
        c = field.shape[-1]
        size = wide * COLS
        field[pl.ds(HALO + row, n), HALO : HALO + wide] = new.reshape(n, wide, COLS, c)
        for r in range(n):
            packed = move(pack1 if which == 1 else pack2, new[r * size : (r + 1) * size])
            packs[which][row + r] = packed.reshape(2, COLS, c)

    def centre(values):
        c = values.shape[-1]
        ones = jnp.full((c, c), 1.0 / c, bf16)
        mean = jnp.dot(values.astype(bf16), ones, preferred_element_type=f32)
        centred = values.astype(f32) - mean
        variance = jnp.dot((centred * centred).astype(bf16), ones, preferred_element_type=f32)
        return (centred * lax.rsqrt(variance + EPSILON)).astype(bf16)

    def gelu_twice(h):
        square = jnp.minimum(h * h, ERF_END)
        q = (ERF_FIT[2] * square + ERF_FIT[1]) * square + ERF_FIT[0]
        return h + h * jnp.tanh(h * q)

    def depthwise(field, taps, sums, layer, row, n):
        wide = field.shape[1] - 2 * HALO
        c = field.shape[-1]

        @pl.loop(0, wide)
        def _(slab):
            for lane in range(c // 128):
                lanes = slice(lane * 128, (lane + 1) * 128)
                stacks = [[] for _ in range(n)]
                for b in range(7):
                    cells = [field[row + r, slab + b, :, lanes] for r in range(n + 2 * HALO)]
                    tap = [taps[layer, 7 * a + b, :, lanes] for a in range(7)]
                    for r in range(n):
                        p = [cells[r + a] * tap[a] for a in range(7)]
                        stacks[r].append(((p[0] + p[1]) + (p[2] + p[3])) + ((p[4] + p[5]) + p[6]))
                        if b in (1, 3, 5):
                            top = stacks[r].pop()
                            stacks[r].append(stacks[r].pop() + top)
                        if b in (3, 6):
                            top = stacks[r].pop()
                            stacks[r].append(stacks[r].pop() + top)
                for r in range(n):
                    sums[r, slab, :, lanes] = stacks[r][0] + stacks[r][1]

        return sums[0:n].reshape(n * wide * COLS, c)

    def branch_rows(field, taps, w_in, w_out, sums, layer, row, n):
        flat = centre(depthwise(field, taps, sums, layer, row, n))
        hidden_size = w_in.shape[-1]
        step = 512
        total = None
        for k in range(0, hidden_size, step):
            h = jnp.dot(flat, w_in[layer, :, k : k + step], preferred_element_type=f32)
            g = gelu_twice(h.astype(bf16))
            part = jnp.dot(g, w_out[layer, k : k + step, :], preferred_element_type=f32)
            total = part if total is None else total + part
        return 0.5 * total

    def plain(field, row, n):
        wide = field.shape[1] - 2 * HALO
        c = field.shape[-1]
        return field[pl.ds(HALO + row, n), HALO : HALO + wide].astype(f32).reshape(n * wide * COLS, c)

    def section_one(layer, row, n):
        field = fields[layer]
        branch = branch_rows(field, kb1, a1, b1, sum1, layer, row, n)
        new = (plain(field, row, n) + branch).astype(bf16)
        if layer == 0:
            store_field(1, row, n, new)
            return
        normed = centre(new.astype(f32)).reshape(n, wide_one, COLS, c_one)
        for r in range(n):
            place = row + r
            first = 2 * lax.rem(place, 2)
            for q in range(wide_one):
                patches[first + q % 2, lax.div(place, 2), q // 2] = normed[r, q]

    def section_two(layer, row, n):
        field = fields[2 + layer]
        branch = branch_rows(field, kb2, a2, b2, sum2, layer, row, n)
        old = plain(field, row, n)
        mark = marks[lax.div(me_row * rows_two, TILE2), lax.div(me_col * (wide_two * COLS), TILE2)]
        keep = jnp.full(old.shape, mark, jnp.int32) == 1
        new = jnp.where(keep, old + branch, old).astype(bf16)
        if layer == 0:
            store_field(3, row, n, new)
            return
        size = wide_two * COLS
        for r in range(n):
            out_ref[row + r] = move(unorder, new[r * size : (r + 1) * size]).reshape(wide_two, COLS, c_two)

    def run(work, which, layer, rows):
        inner = rows - 2 * HALO
        per_step = largest_divisor(inner, 5)
        unroll = largest_divisor(rows, 4)
        arrive(which, (2, 3))

        @pl.loop(0, rows // unroll)
        def _(index):
            for r in range(unroll):
                fill(which, HALO + index * unroll + r)

        @pl.loop(0, inner // per_step)
        def _(index):
            work(layer, HALO + index * per_step, per_step)

        arrive(which, (0, 1, 4, 5, 6, 7))

        @pl.loop(0, 2)
        def _(index):
            for r in range(HALO):
                fill(which, index * (HALO + rows) + r)
            work(layer, index * (rows - HALO), HALO)

    loads[1].wait()
    spread_taps(kb1, t1)
    loads[0].wait()
    loads[2].wait()
    loads[3].wait()
    run(section_one, 0, 0, rows_one)
    send(1)
    loads[5].wait()
    spread_taps(kb2, t2)
    run(section_one, 1, 1, rows_one)

    loads[4].wait()
    together = largest_divisor(rows_two, 4)

    @pl.loop(0, rows_two // together)
    def _(index):
        total = None
        for q in range(4):
            patch = patches[q, pl.ds(index * together, together)].reshape(together * wide_two * COLS, c_one)
            part = jnp.dot(patch, sk[q * c_one : (q + 1) * c_one], preferred_element_type=f32)
            total = part if total is None else total + part
        store_field(2, index * together, together, total.astype(bf16))

    send(2)
    loads[6].wait()
    loads[7].wait()
    run(section_two, 2, 0, rows_two)
    send(3)
    run(section_two, 3, 1, rows_two)
    for which in range(4):
        sent(which)


def per_device(
    count_rows,
    count_cols,
    input_picture,
    spatial_taps_first,
    widening_matrix_first,
    narrowing_matrix_first,
    stride_kernel_matrix,
    spatial_taps_second,
    widening_matrix_second,
    narrowing_matrix_second,
    sky_clarity_marks,
):
    rows, cols, c_one = input_picture.shape
    c_two = stride_kernel_matrix.shape[1]
    half = rows // 2
    wide_one = cols // COLS
    wide_two = cols // (2 * COLS)
    weights = (
        spatial_taps_first.transpose(1, 0, 2), widening_matrix_first, narrowing_matrix_first,
        stride_kernel_matrix,
        spatial_taps_second.transpose(1, 0, 2), widening_matrix_second, narrowing_matrix_second,
    )
    vmem = pltpu.VMEM
    field_one = (rows + 2 * HALO, wide_one + 2 * HALO, COLS, c_one)
    field_two = (half + 2 * HALO, wide_two + 2 * HALO, COLS, c_two)
    layers = spatial_taps_first.shape[0]
    shapes = [
        (rows + 2 * HALO, wide_one + 2, COLS, c_one),
        field_one, field_one, field_two, field_two,
        (rows + 2 * HALO, 2, COLS, c_one),
        (half + 2 * HALO, 2, COLS, c_two),
        (half + 2 * HALO, 2, COLS, c_two),
        (rows, 2, COLS, c_one),
        (half, 2, COLS, c_two),
        (half, 2, COLS, c_two),
        *[w.shape for w in weights],
        (layers, 49, COLS, c_one),
        (layers, 49, COLS, c_two),
        (5, wide_one, COLS, c_one),
        (5, wide_two, COLS, c_two),
        ((wide_one + 2 * HALO) * COLS, (wide_one + 2) * COLS),
        (2 * HALO * COLS, (wide_one + 2) * COLS),
        (2 * HALO * COLS, (wide_two + 2) * COLS),
        (2 * COLS, wide_one * COLS),
        (2 * COLS, wide_two * COLS),
        (wide_two * COLS, wide_two * COLS),
        (4, half, wide_two, COLS, c_one),
    ]
    out = pl.pallas_call(
        functools.partial(kernel, count_rows, count_cols),
        out_shape=jax.ShapeDtypeStruct((half, wide_two, COLS, c_two), bf16),
        in_specs=[pl.BlockSpec(memory_space=pl.ANY)] * 8 + [pl.BlockSpec(memory_space=pltpu.SMEM)],
        out_specs=pl.BlockSpec(memory_space=vmem),
        scratch_shapes=[
            *[vmem(shape, bf16) for shape in shapes],
            pltpu.SemaphoreType.DMA((8,)),
            pltpu.SemaphoreType.DMA((4, len(SIDES))),
            pltpu.SemaphoreType.DMA((4, len(SIDES))),
        ],
        compiler_params=pltpu.CompilerParams(
            collective_id=0, has_side_effects=True, vmem_limit_bytes=60 * 2**20
        ),
        name="sections",
    )(input_picture.reshape(rows, wide_one, COLS, c_one), *weights, sky_clarity_marks)
    return out.reshape(half, cols // 2, c_two)


def solution(mesh):
    placed = (P("row", "col", None), P(), P(), P(), P(), P(), P(), P(), P())
    return jax.shard_map(
        functools.partial(per_device, mesh.shape["row"], mesh.shape["col"]),
        mesh=mesh, in_specs=placed, out_specs=P("row", "col", None), check_vma=False,
    )
```

time: 98 us -> 88 us (0.90)
  Pallas kernels: 90.3 us -> 85.9 us
  local copies, waits for them, and re-layouts: 5.46 us -> 1.87 us
  other arithmetic: 1.24 us -> 0 us
    pallas_call x1, Pallas kernels: 90.3 us -> 85.9 us  [per_device(): pl.pallas_call(functools.partial(kernel, count_rows, count_cols), out_sha...]
    unnamed x3 -> x1, local copies, waits for them, and re-layouts: 4.87 us -> 1.87 us
    eq x1 -> x0, other arithmetic: 1.24 us -> none  [per_device(): flag = jnp.broadcast_to((flag == 1).astype(f32), (8, c_two))]
where the time goes in v1:
time: 88 us; the launch traced here: 87.8 us
  Pallas kernels  85.9 us (98%)
  local copies, waits for them, and re-layouts  1.87 us (2%)
    pallas_call x1, Pallas kernels, per_device(): pl.pallas_call(functools.partial(kernel, count_rows, count_cols), out_sha...  85.9 us
    unnamed x1, local copies, waits for them, and re-layouts  1.87 us

profile of v1, /device:TPU:11, one launch (start us, length us, event | category | flops | bytes accessed | tf_op | source)
XLA Modules:
  0.0 87.8 jit_solution(11886886387964749243)
XLA Ops:
  0.0 85.9 %sections.1 = bf16[8,4,16,512]{3,2,1,0:T(8,128)(2,1)} custom-call(bf16[16,8,16,256]{3,2,1,0:T(8,128)(2,1)} %bitcast.5, bf16[49,2,256]{2,1,0:T(2,128)(2,1)} %bitcast.7, bf16[2,256,1024]{2,1,0:T(8,128)(2,1)} %a1_hbm.1, bf16[2,1024,256]{2,1,0:T(8,128)(2,1)} %b1_hbm.1, bf16[1024,512]{1,0:T(8,128)(2,1)} %sk_hbm.1, bf16[49,2,512]{2,1,0:T(2,128)(2,1)} %bitcast.6, ...), custom_call_target="tpu_custom_call" | custom-call | tf_op jit(solution)/shard_map/sections/pallas_call | solution.py:424
  86.0 1.9 %copy.11 = bf16[8,64,512]{2,1,0:T(8,128)(2,1)} copy(bf16[8,64,512]{2,1,0:T(8,128)(2,1)} %bitcast.4) | data formatting | bytes 1048576

commit v2 on v1

--- a/solution.py
+++ b/solution.py
@@ -14,6 +14,14 @@
 ERF_FIT = (0.7975078823814434, 0.037005647651999776, -0.00035151703937969365)
 ERF_END = 25.0
 SIDES = ((-1, 0), (1, 0), (0, -1), (0, 1), (-1, -1), (-1, 1), (1, -1), (1, 1))
+TOP, INNER, BOTTOM = range(3)
+MESSAGES = (
+    (-1, 0, None), (-1, -1, None), (-1, 1, None),
+    (1, 0, None), (1, -1, None), (1, 1, None),
+    (0, -1, TOP), (0, 1, TOP), (0, -1, INNER), (0, 1, INNER), (0, -1, BOTTOM), (0, 1, BOTTOM),
+)
+UPWARD, DOWNWARD = (0, 1, 2), (3, 4, 5)
+EDGES = ((6, 7), (8, 9), (10, 11))
 f32 = jnp.float32
 bf16 = jnp.bfloat16
 
@@ -80,13 +88,15 @@
         total = total + jnp.where(near, 1, 0)
     pl.semaphore_wait(barrier, total)
 
-    def transfer(which, side):
-        dr, dc = SIDES[side]
+    def transfer(which, message):
+        dr, dc, part = MESSAGES[message]
         rows = fields[which].shape[0] - 2 * HALO
         wide = fields[which].shape[1] - 2 * HALO
-        from_row = {-1: 0, 0: 0, 1: rows - HALO}[dr]
-        to_row = {-1: HALO + rows, 0: HALO, 1: 0}[dr]
-        n_rows = HALO if dr else rows
+        if dr:
+            from_row, to_row, n_rows = {-1: (0, HALO + rows, HALO), 1: (rows - HALO, 0, HALO)}[dr]
+        else:
+            from_row = (0, HALO, rows - HALO)[part]
+            to_row, n_rows = HALO + from_row, (HALO, rows - 2 * HALO, HALO)[part]
         if which == 0:
             from_block = {-1: 0, 0: 0, 1: wide - 1}[dc]
             to_block = {-1: wide + 1, 0: 1, 1: 0}[dc]
@@ -102,8 +112,8 @@
         return pltpu.make_async_remote_copy(
             src_ref=src,
             dst_ref=dst,
-            send_sem=send_sem.at[which, side],
-            recv_sem=recv_sem.at[which, side],
+            send_sem=send_sem.at[which, message],
+            recv_sem=recv_sem.at[which, message],
             device_id=(
                 jnp.clip(me_row + dr, 0, count_rows - 1),
                 jnp.clip(me_col + dc, 0, count_cols - 1),
@@ -111,27 +121,41 @@
             device_id_type=pl.DeviceIdType.MESH,
         )
 
-    def send(which):
-        for side in (2, 3, 0, 1, 4, 5, 6, 7):
-            @pl.when(exists(*SIDES[side]))
-            def _(side=side):
-                transfer(which, side).start()
-
-    def arrive(which, sides):
-        for side in sides:
-            dr, dc = SIDES[side]
+    def send(which, messages):
+        for message in messages:
+            @pl.when(exists(*MESSAGES[message][:2]))
+            def _(message=message):
+                transfer(which, message).start()
+
+    def arrive(which, messages):
+        for message in messages:
+            dr, dc, _ = MESSAGES[message]
 
             @pl.when(exists(-dr, -dc))
-            def _(side=side):
-                transfer(which, side).wait_recv()
+            def _(message=message):
+                transfer(which, message).wait_recv()
 
     def sent(which):
-        for side in range(len(SIDES)):
-            @pl.when(exists(*SIDES[side]))
-            def _(side=side):
-                transfer(which, side).wait_send()
-
-    send(0)
+        for message in range(len(MESSAGES)):
+            @pl.when(exists(*MESSAGES[message][:2]))
+            def _(message=message):
+                transfer(which, message).wait_send()
+
+    def by_side(side, act, if_top, if_bottom):
+        @pl.when(side == 0)
+        def _():
+            act(if_top)
+
+        @pl.when(side == 1)
+        def _():
+            act(if_bottom)
+
+    early = 1 - lax.rem(me_row, 2)
+    late = 1 - early
+
+    send(0, EDGES[INNER])
+    for side in (early, late):
+        by_side(side, functools.partial(send, 0), EDGES[TOP] + UPWARD, EDGES[BOTTOM] + DOWNWARD)
 
     for field, left, right, inner in (
         (natural, 0, wide_one + 1, None),
@@ -316,58 +340,93 @@
         for r in range(n):
             out_ref[row + r] = move(unorder, new[r * size : (r + 1) * size]).reshape(wide_two, COLS, c_two)
 
-    def run(work, which, layer, rows):
+    def coarse(row, n):
+        total = None
+        for q in range(4):
+            patch = patches[q, pl.ds(row, n)].reshape(n * wide_two * COLS, c_one)
+            part = jnp.dot(patch, sk[q * c_one : (q + 1) * c_one], preferred_element_type=f32)
+            total = part if total is None else total + part
+        store_field(2, row, n, total.astype(bf16))
+
+    def run(work, which, layer, rows, after_inner, after_border):
         inner = rows - 2 * HALO
         per_step = largest_divisor(inner, 5)
-        unroll = largest_divisor(rows, 4)
-        arrive(which, (2, 3))
-
-        @pl.loop(0, rows // unroll)
+        steps = inner // per_step
+        free_steps = max(0, steps + (-HALO // per_step))
+
+        def border_edges(side):
+            by_side(side, functools.partial(arrive, which), EDGES[TOP], EDGES[BOTTOM])
+            for r in range(HALO):
+                fill(which, HALO + side * (rows - HALO) + r)
+
+        arrive(which, EDGES[INNER])
+
+        @pl.loop(0, steps)
         def _(index):
-            for r in range(unroll):
-                fill(which, HALO + index * unroll + r)
-
-        @pl.loop(0, inner // per_step)
+            for r in range(per_step):
+                fill(which, 2 * HALO + index * per_step + r)
+
+        border_edges(early)
+
+        @pl.loop(0, steps)
         def _(index):
-            work(layer, HALO + index * per_step, per_step)
-
-        arrive(which, (0, 1, 4, 5, 6, 7))
+            @pl.when(index == free_steps)
+            def _():
+                border_edges(late)
+
+            place = early * (steps - 1 - index) + late * index
+            work(layer, HALO + place * per_step, per_step)
+
+        after_inner()
 
         @pl.loop(0, 2)
-        def _(index):
+        def _(phase):
+            side = lax.rem(phase + early, 2)
+            by_side(side, functools.partial(arrive, which), DOWNWARD, UPWARD)
             for r in range(HALO):
-                fill(which, index * (HALO + rows) + r)
-            work(layer, index * (rows - HALO), HALO)
+                fill(which, side * (HALO + rows) + r)
+            work(layer, side * (rows - HALO), HALO)
+            after_border(side)
+
+    def send_inner(which):
+        send(which, EDGES[INNER])
+
+    def send_border(which, side):
+        by_side(side, functools.partial(send, which), EDGES[TOP] + UPWARD, EDGES[BOTTOM] + DOWNWARD)
 
     loads[1].wait()
     spread_taps(kb1, t1)
-    loads[0].wait()
-    loads[2].wait()
-    loads[3].wait()
-    run(section_one, 0, 0, rows_one)
-    send(1)
     loads[5].wait()
     spread_taps(kb2, t2)
-    run(section_one, 1, 1, rows_one)
-
-    loads[4].wait()
-    together = largest_divisor(rows_two, 4)
-
-    @pl.loop(0, rows_two // together)
-    def _(index):
-        total = None
-        for q in range(4):
-            patch = patches[q, pl.ds(index * together, together)].reshape(together * wide_two * COLS, c_one)
-            part = jnp.dot(patch, sk[q * c_one : (q + 1) * c_one], preferred_element_type=f32)
-            total = part if total is None else total + part
-        store_field(2, index * together, together, total.astype(bf16))
-
-    send(2)
+    for index in (0, 2, 3, 4):
+        loads[index].wait()
+    run(
+        section_one, 0, 0, rows_one,
+        functools.partial(send_inner, 1), functools.partial(send_border, 1),
+    )
+
+    def coarse_inner():
+        inner = rows_two - 2 * HALO
+        together = largest_divisor(inner, 4)
+
+        @pl.loop(0, inner // together)
+        def _(index):
+            coarse(HALO + index * together, together)
+
+        send_inner(2)
+
+    def coarse_border(side):
+        coarse(side * (rows_two - HALO), HALO)
+        send_border(2, side)
+
+    run(section_one, 1, 1, rows_one, coarse_inner, coarse_border)
     loads[6].wait()
     loads[7].wait()
-    run(section_two, 2, 0, rows_two)
-    send(3)
-    run(section_two, 3, 1, rows_two)
+    run(
+        section_two, 2, 0, rows_two,
+        functools.partial(send_inner, 3), functools.partial(send_border, 3),
+    )
+    run(section_two, 3, 1, rows_two, lambda: None, lambda side: None)
     for which in range(4):
         sent(which)
 
@@ -429,8 +488,8 @@
         scratch_shapes=[
             *[vmem(shape, bf16) for shape in shapes],
             pltpu.SemaphoreType.DMA((8,)),
-            pltpu.SemaphoreType.DMA((4, len(SIDES))),
-            pltpu.SemaphoreType.DMA((4, len(SIDES))),
+            pltpu.SemaphoreType.DMA((4, len(MESSAGES))),
+            pltpu.SemaphoreType.DMA((4, len(MESSAGES))),
         ],
         compiler_params=pltpu.CompilerParams(
             collective_id=0, has_side_effects=True, vmem_limit_bytes=60 * 2**20

time: 88 us -> 78.8 us (0.90); the launches traced: 87.8 us -> 77.4 us
  Pallas kernels: 85.9 us -> 75.5 us
    pallas_call x1, Pallas kernels: 85.9 us -> 75.5 us  [per_device(): pl.pallas_call(functools.partial(kernel, count_rows, count_cols), out_sha...]
where the time goes in v2:
time: 78.8 us; the launch traced here: 77.4 us
  Pallas kernels  75.5 us (96%)
  local copies, waits for them, and re-layouts  1.87 us (2%)
    pallas_call x1, Pallas kernels, per_device(): pl.pallas_call(functools.partial(kernel, count_rows, count_cols), out_sha...  75.5 us
    unnamed x1, local copies, waits for them, and re-layouts  1.87 us

profile of v2, /device:TPU:11, one launch (start us, length us, event | category | flops | bytes accessed | tf_op | source)
XLA Modules:
  0.0 77.4 jit_solution(6543391691890810253)
XLA Ops:
  0.0 75.5 %sections.1 = bf16[8,4,16,512]{3,2,1,0:T(8,128)(2,1)} custom-call(bf16[16,8,16,256]{3,2,1,0:T(8,128)(2,1)} %bitcast.5, bf16[49,2,256]{2,1,0:T(2,128)(2,1)} %bitcast.7, bf16[2,256,1024]{2,1,0:T(8,128)(2,1)} %a1_hbm.1, bf16[2,1024,256]{2,1,0:T(8,128)(2,1)} %b1_hbm.1, bf16[1024,512]{1,0:T(8,128)(2,1)} %sk_hbm.1, bf16[49,2,512]{2,1,0:T(2,128)(2,1)} %bitcast.6, ...), custom_call_target="tpu_custom_call" | custom-call | tf_op jit(solution)/shard_map/sections/pallas_call | solution.py:483
  75.5 1.9 %copy.11 = bf16[8,64,512]{2,1,0:T(8,128)(2,1)} copy(bf16[8,64,512]{2,1,0:T(8,128)(2,1)} %bitcast.4) | data formatting | bytes 1048576

commit v3 on v2

--- a/solution.py
+++ b/solution.py
@@ -11,6 +11,7 @@
 EPSILON = 1e-06
 HALO = 3
 COLS = 16
+LANES = 128
 ERF_FIT = (0.7975078823814434, 0.037005647651999776, -0.00035151703937969365)
 ERF_END = 25.0
 SIDES = ((-1, 0), (1, 0), (0, -1), (0, 1), (-1, -1), (-1, 1), (1, -1), (1, 1))
@@ -28,6 +29,14 @@
 
 def largest_divisor(number, limit):
     return next(d for d in range(limit, 0, -1) if number % d == 0)
+
+
+def lane_groups(count):
+    return [slice(g * LANES, (g + 1) * LANES) for g in range(count)]
+
+
+def joined(pieces):
+    return jnp.concatenate([p.reshape(-1, LANES) for p in pieces], axis=1)
 
 
 def kernel(
@@ -48,8 +57,8 @@
     rows_two = e2.shape[0] - 2 * HALO
     wide_one = e0.shape[1] - 2 * HALO
     wide_two = e2.shape[1] - 2 * HALO
-    c_one = e0.shape[-1]
-    c_two = e2.shape[-1]
+    c_one = e0.shape[2] * LANES
+    c_two = e2.shape[2] * LANES
     me_row = lax.axis_index("row")
     me_col = lax.axis_index("col")
 
@@ -230,28 +239,34 @@
         for tap in range(49):
             both = src[tap].astype(f32)
             for layer in range(both.shape[0]):
-                dst[layer, tap] = jnp.broadcast_to(both[layer : layer + 1], dst.shape[2:]).astype(bf16)
+                for g, lanes in enumerate(lane_groups(dst.shape[2])):
+                    dst[layer, tap, g] = jnp.broadcast_to(both[layer : layer + 1, lanes], (COLS, LANES)).astype(bf16)
 
     def fill(which, row):
         field = fields[which]
         wide = field.shape[1] - 2 * HALO
-        c = field.shape[-1]
+        groups = lane_groups(field.shape[2])
+        c = len(groups) * LANES
         if which == 0:
-            values = natural[row].reshape((wide + 2) * COLS, c)
-            field[row] = move(order0, values).reshape(wide + 2 * HALO, COLS, c)
+            whole = move(order0, natural[row].reshape((wide + 2) * COLS, c))
+            for g, lanes in enumerate(groups):
+                field[row, :, g] = whole[:, lanes].reshape(wide + 2 * HALO, COLS, LANES)
             return
-        inner = field[row, HALO : HALO + wide].reshape(wide * COLS, c)
+        inner = joined([field[row, HALO : HALO + wide, g] for g in range(len(groups))])
         values = jnp.concatenate([inner, edges[which][row].reshape(2 * COLS, c)], axis=0)
-        outer = move(fill1 if which == 1 else fill2, values).reshape(2 * HALO, COLS, c)
-        field[row, 0:HALO] = outer[:HALO]
-        field[row, HALO + wide : 2 * HALO + wide] = outer[HALO:]
+        outer = move(fill1 if which == 1 else fill2, values)
+        for g, lanes in enumerate(groups):
+            part = outer[:, lanes].reshape(2 * HALO, COLS, LANES)
+            field[row, 0:HALO, g] = part[:HALO]
+            field[row, HALO + wide : 2 * HALO + wide, g] = part[HALO:]
 
     def store_field(which, row, n, new):
         field = fields[which]
         wide = field.shape[1] - 2 * HALO
-        c = field.shape[-1]
+        c = field.shape[2] * LANES
         size = wide * COLS
-        field[pl.ds(HALO + row, n), HALO : HALO + wide] = new.reshape(n, wide, COLS, c)
+        for g, lanes in enumerate(lane_groups(field.shape[2])):
+            field[pl.ds(HALO + row, n), HALO : HALO + wide, g] = new[:, lanes].reshape(n, wide, COLS, LANES)
         for r in range(n):
             packed = move(pack1 if which == 1 else pack2, new[r * size : (r + 1) * size])
             packs[which][row + r] = packed.reshape(2, COLS, c)
@@ -271,16 +286,15 @@
 
     def depthwise(field, taps, sums, layer, row, n):
         wide = field.shape[1] - 2 * HALO
-        c = field.shape[-1]
+        groups = field.shape[2]
 
         @pl.loop(0, wide)
         def _(slab):
-            for lane in range(c // 128):
-                lanes = slice(lane * 128, (lane + 1) * 128)
+            for g in range(groups):
                 stacks = [[] for _ in range(n)]
                 for b in range(7):
-                    cells = [field[row + r, slab + b, :, lanes] for r in range(n + 2 * HALO)]
-                    tap = [taps[layer, 7 * a + b, :, lanes] for a in range(7)]
+                    cells = [field[row + r, slab + b, g] for r in range(n + 2 * HALO)]
+                    tap = [taps[layer, 7 * a + b, g] for a in range(7)]
                     for r in range(n):
                         p = [cells[r + a] * tap[a] for a in range(7)]
                         stacks[r].append(((p[0] + p[1]) + (p[2] + p[3])) + ((p[4] + p[5]) + p[6]))
@@ -291,9 +305,9 @@
                             top = stacks[r].pop()
                             stacks[r].append(stacks[r].pop() + top)
                 for r in range(n):
-                    sums[r, slab, :, lanes] = stacks[r][0] + stacks[r][1]
-
-        return sums[0:n].reshape(n * wide * COLS, c)
+                    sums[r, slab, g] = stacks[r][0] + stacks[r][1]
+
+        return joined([sums[0:n, :, g] for g in range(groups)])
 
     def branch_rows(field, taps, w_in, w_out, sums, layer, row, n):
         flat = centre(depthwise(field, taps, sums, layer, row, n))
@@ -309,8 +323,8 @@
 
     def plain(field, row, n):
         wide = field.shape[1] - 2 * HALO
-        c = field.shape[-1]
-        return field[pl.ds(HALO + row, n), HALO : HALO + wide].astype(f32).reshape(n * wide * COLS, c)
+        pieces = [field[pl.ds(HALO + row, n), HALO : HALO + wide, g] for g in range(field.shape[2])]
+        return joined(pieces).astype(f32)
 
     def section_one(layer, row, n):
         field = fields[layer]
@@ -455,8 +469,8 @@
         spatial_taps_second.transpose(1, 0, 2), widening_matrix_second, narrowing_matrix_second,
     )
     vmem = pltpu.VMEM
-    field_one = (rows + 2 * HALO, wide_one + 2 * HALO, COLS, c_one)
-    field_two = (half + 2 * HALO, wide_two + 2 * HALO, COLS, c_two)
+    field_one = (rows + 2 * HALO, wide_one + 2 * HALO, c_one // LANES, COLS, LANES)
+    field_two = (half + 2 * HALO, wide_two + 2 * HALO, c_two // LANES, COLS, LANES)
     layers = spatial_taps_first.shape[0]
     shapes = [
         (rows + 2 * HALO, wide_one + 2, COLS, c_one),
@@ -468,10 +482,10 @@
         (half, 2, COLS, c_two),
         (half, 2, COLS, c_two),
         *[w.shape for w in weights],
-        (layers, 49, COLS, c_one),
-        (layers, 49, COLS, c_two),
-        (5, wide_one, COLS, c_one),
-        (5, wide_two, COLS, c_two),
+        (layers, 49, c_one // LANES, COLS, LANES),
+        (layers, 49, c_two // LANES, COLS, LANES),
+        (5, wide_one, c_one // LANES, COLS, LANES),
+        (5, wide_two, c_two // LANES, COLS, LANES),
         ((wide_one + 2 * HALO) * COLS, (wide_one + 2) * COLS),
         (2 * HALO * COLS, (wide_one + 2) * COLS),
         (2 * HALO * COLS, (wide_two + 2) * COLS),

time: 78.8 us -> 79.7 us (1.011)
  Pallas kernels: 75.5 us -> 76.6 us
    pallas_call x1, Pallas kernels: 75.5 us -> 76.6 us  [per_device(): pl.pallas_call(functools.partial(kernel, count_rows, count_cols), out_sha...]
where the time goes in v3:
time: 79.7 us; the launch traced here: 78.5 us
  Pallas kernels  76.6 us (96%)
  local copies, waits for them, and re-layouts  1.87 us (2%)
    pallas_call x1, Pallas kernels, per_device(): pl.pallas_call(functools.partial(kernel, count_rows, count_cols), out_sha...  76.6 us
    unnamed x1, local copies, waits for them, and re-layouts  1.87 us

profile of v3, /device:TPU:11, one launch (start us, length us, event | category | flops | bytes accessed | tf_op | source)
XLA Modules:
  0.0 78.5 jit_solution(12213703451342502048)
XLA Ops:
  0.0 76.6 %sections.1 = bf16[8,4,16,512]{3,2,1,0:T(8,128)(2,1)} custom-call(bf16[16,8,16,256]{3,2,1,0:T(8,128)(2,1)} %bitcast.5, bf16[49,2,256]{2,1,0:T(2,128)(2,1)} %bitcast.7, bf16[2,256,1024]{2,1,0:T(8,128)(2,1)} %a1_hbm.1, bf16[2,1024,256]{2,1,0:T(8,128)(2,1)} %b1_hbm.1, bf16[1024,512]{1,0:T(8,128)(2,1)} %sk_hbm.1, bf16[49,2,512]{2,1,0:T(2,128)(2,1)} %bitcast.6, ...), custom_call_target="tpu_custom_call" | custom-call | tf_op jit(solution)/shard_map/sections/pallas_call | solution.py:497
  76.6 1.9 %copy.11 = bf16[8,64,512]{2,1,0:T(8,128)(2,1)} copy(bf16[8,64,512]{2,1,0:T(8,128)(2,1)} %bitcast.4) | data formatting | bytes 1048576
